TPU v7x, 32 devices: a whole 2x2x4 slice. The times are simulated.
32 devices in a mesh: win: 2 (over x), chan: 4 (over y, core), tm: 4 (over z).
Axes of the slice: x: 2, y: 2, z: 4, core: 2. Of those that a mesh axis runs over, the one named last changes fastest.
Arguments:
- samples: bfloat16 [256, 65536], P(('win', 'chan'), 'tm'), parts along dimension 0, may hold values from -6 to 6
- gap_start: int32 [256, 4], P(('win', 'chan')), parts along dimension 0, may hold values from 0 to 255, as said below
- gap_len: int32 [256, 4], P(('win', 'chan')), parts along dimension 0, may hold values from 0 to 16, as said below
- offsets: int32 [32], replicated, may hold values from -32 to 32, as said below
Outputs:
- correlation: float32 [32, 256, 1024], P('tm', ('win', 'chan')), parts along dimension 1
There are 2 independent parts, one for each index of `win`. A program takes and returns all parts, laid end to end along the dimension named above; an argument that names none is the same for every part. Nothing has to cross between parts.
Inputs may be any that keep to these rules, and one draw needn't show every extreme that they name: `gap_start`: A gap may intersection others and run past the window's end. `gap_len`: A length of 0 is no gap; some channels carry far longer gaps than others. 32 distinct nonzero offsets; both -32 and 32 are among them.
All inputs are finite; a program needn't handle non-finite values.
Results may differ from a plain program's by a relative error of at most 0.0056.
Values may be sent and summed in bfloat16 or wider, within the bound.
A program may use at most 128 MiB of HBM per device.

v0:
```python
import math

import jax
import jax.numpy as jnp
from jax import lax
from jax.sharding import PartitionSpec as P

NFFT = 2048
LAGS = 1024
R = 32
BAND = 64
BLK = 256


def shifted(value, axis, steps):
    count = lax.axis_size(axis)
    first, last = (max(0, -steps), min(count, count - steps))
    return lax.ppermute(value, axis, [(source, source + steps) for source in range(first, last)])


def padded(block, sides, width):
    for axis, dim in sides:
        count = lax.axis_size(axis)
        forward = [(i, i + 1) for i in range(count - 1)]
        backward = [(target, source) for source, target in forward]
        low = lax.ppermute(
            lax.slice_in_dim(block, block.shape[dim] - width, None, axis=dim), axis, forward
        )
        high = lax.ppermute(lax.slice_in_dim(block, 0, width, axis=dim), axis, backward)
        block = jnp.concatenate([low, block, high], axis=dim)
    return block


def dft_table():
    rows = jnp.arange(NFFT, dtype=jnp.int32)[:, None]
    freqs = jnp.arange(NFFT // 2, dtype=jnp.int32)[None, :]
    phase = (rows * freqs % NFFT).astype(jnp.float32) * (2.0 * math.pi / NFFT)
    return jnp.concatenate([jnp.cos(phase), -jnp.sin(phase)], axis=1).astype(jnp.bfloat16)


def lag_table(segments):
    freqs = jnp.arange(NFFT // 2, dtype=jnp.int32)[:, None]
    shifts = jnp.arange(LAGS, dtype=jnp.int32)[None, :] - LAGS // 2
    phase = jnp.mod(freqs * shifts, NFFT).astype(jnp.float32) * (2.0 * math.pi / NFFT)
    weight = jnp.where(freqs == 0, 1.0, 2.0).astype(jnp.float32) / jnp.sqrt(
        jnp.float32(NFFT * segments)
    )
    return jnp.concatenate([weight * jnp.cos(phase), -weight * jnp.sin(phase)], axis=0)


def whiten(spectrum, half_len):
    real_part = spectrum[..., :half_len]
    imag_part = spectrum[..., half_len:]
    power = real_part * real_part + imag_part * imag_part
    band_power = jnp.mean(power.reshape(power.shape[:-1] + (half_len // BAND, BAND)), axis=-1)
    factor = jnp.repeat(1.0 / jnp.sqrt(band_power + 1e-06), BAND, axis=-1)
    return jnp.concatenate([real_part * factor, imag_part * factor], axis=-1).astype(jnp.bfloat16)


def shards(samples, gap_start, gap_len, offsets):
    channels, local_len = samples.shape
    half_len = NFFT // 2
    seg_count = local_len // half_len
    tm_count = lax.axis_size("tm")
    slot_rows = offsets.shape[0] // tm_count
    following = shifted(samples[:, :half_len], "tm", -1)
    extended = jnp.concatenate([samples, following], axis=1)
    blocks = (
        lax.axis_index("tm") * local_len + jnp.arange(local_len + half_len, dtype=jnp.int32)
    ) // BLK
    covered = jnp.any(
        (blocks[None, None, :] >= gap_start[:, :, None])
        & (blocks[None, None, :] < (gap_start + gap_len)[:, :, None]),
        axis=1,
    )
    masked = jnp.where(covered, jnp.zeros_like(extended), extended)
    pieces = masked.reshape(channels, seg_count + 1, half_len)
    frames = jnp.concatenate([pieces[:, :-1], pieces[:, 1:]], axis=2)
    taper = 0.5 - 0.5 * jnp.cos(
        jnp.arange(NFFT, dtype=jnp.int32).astype(jnp.float32) * (2.0 * math.pi / NFFT)
    )
    tapered = (frames.astype(jnp.float32) * taper).astype(jnp.bfloat16)
    spectrum = jnp.dot(
        tapered.reshape(channels * seg_count, NFFT), dft_table(), preferred_element_type=jnp.float32
    )
    whitened = whiten(spectrum.reshape(channels, seg_count, NFFT), half_len)
    widened = padded(whitened, (("chan", 0),), R)
    lags = lag_table(seg_count * tm_count)

    def one_slot(shift_by):
        partner = lax.dynamic_slice_in_dim(widened, R + shift_by, channels, 0)
        real_own = whitened[..., :half_len].astype(jnp.float32)
        imag_own = whitened[..., half_len:].astype(jnp.float32)
        real_far = partner[..., :half_len].astype(jnp.float32)
        imag_far = partner[..., half_len:].astype(jnp.float32)
        real_sum = jnp.sum(real_own * real_far + imag_own * imag_far, axis=1)
        imag_sum = jnp.sum(imag_own * real_far - real_own * imag_far, axis=1)
        return jnp.concatenate([real_sum, imag_sum], axis=-1)

    stack = lax.map(one_slot, offsets)
    folded = jnp.dot(
        stack.reshape(lax.axis_size("tm") * slot_rows * channels, NFFT),
        lags,
        precision=lax.Precision.HIGHEST,
        preferred_element_type=jnp.float32,
    )
    return lax.psum_scatter(
        folded.reshape(lax.axis_size("tm") * slot_rows, channels, LAGS),
        "tm",
        scatter_dimension=0,
        tiled=True,
    )


def solution(mesh):
    placed = (P(("win", "chan"), "tm"), P(("win", "chan"), None), P(("win", "chan"), None), P())
    return jax.shard_map(
        shards,
        mesh=mesh,
        in_specs=placed,
        out_specs=P("tm", ("win", "chan"), None),
        check_vma=False,
    )
```

profile of v0, /device:TPU:0, one launch (start us, length us, event | category | flops | bytes accessed | tf_op | source)
XLA Modules:
  0.0 413.2 jit_solution(3341453205657740871)
XLA Ops:
  8.8 35.0 %negate_convert_fusion = (bf16[2048,1024]{1,0:T(8,128)(2,1)}, bf16[2048,1024]{1,0:T(8,128)(2,1)}) fusion(), kind=kLoop, calls=%fused_computation.25 | loop fusion | flops 35651584 | bytes 8388608 | tf_op jit(solution)/shard_map/convert.3
  43.9 3.2 and_reduce_fusion
  50.3 6.7 %fusion.8 = f32[32,16,2048]{2,1,0:T(8,128)S(1)} fusion(bf16[2048,1024]{1,0:T(8,128)(2,1)S(1)} %copy-done.3, bf16[2048,1024]{1,0:T(8,128)(2,1)} %get-tuple-element.90, bf16[32,16,1024]{2,1,0:T(8,128)(2,1)S(1)} %get-tuple-element.86, bf16[32,16,1024]{2,1,0:T(8,128)(2,1)S(1)} %get-tuple-element.85, f32[2048]{0:T(1024)S(1)} %multiply_subtract_fusion), kind=kOutput, calls=%fused_computation.18 | convolution fusion | flops 4318035968 | bytes 14688256 | tf_op jit(solution)/shard_map/dot_general | solution.py:83
  62.2 3.4 reduce_sum.33
  68.2 3.5 reshape.80
  75.7 3.7 collective-permute-start.1
  80.7 18.0 %cosine_multiply_fusion = (f32[1024,1024]{1,0:T(8,128)}, f32[1024,1024]{1,0:T(8,128)}) fusion(s32[1024]{0:T(1024)S(1)} %iota_add_fusion.1, f32[1024]{0:T(1024)S(1)} %get-tuple-element.91, f32[1024]{0:T(1024)S(1)} %get-tuple-element.92), kind=kLoop, calls=%fused_computation.38 | loop fusion | flops 16777216 | bytes 8400896 | tf_op jit(solution)/shard_map/mul | solution.py:48
  98.7 5.9 %pad_maximum_fusion = bf16[96,16,2048]{2,1,0:T(8,128)(2,1)} fusion(bf16[32,16,2048]{2,1,0:T(8,128)(2,1)} %collective-permute-done.2, bf16[32,16,1024]{2,1,0:T(8,128)(2,1)S(1)} %copy-done.2, bf16[32,16,1024]{2,1,0:T(8,128)(2,1)S(1)} %get-tuple-element.83, bf16[32,16,2048]{2,1,0:T(8,128)(2,1)} %collective-permute-done.1), kind=kLoop, calls=%fused_computation.30 | loop fusion | flops 25165824 | bytes 12582912 | tf_op jit(solution)/shard_map/concatenate | solution.py:30
  104.6 181.7 %while.12 = (s32[]{:T(128)}, f32[32,32,2048]{2,1,0:T(8,128)}, bf16[32,16,2048]{2,1,0:T(8,128)(2,1)S(1)}, s32[32]{0:T(128)S(1)}, bf16[96,16,2048]{2,1,0:T(8,128)(...) while((s32[]{:T(128)}, f32[32,32,2048]{2,1,0:T(8,128)}, ...), condition=%wide.region_5.6_spmd, body=%wide.region_2.5_spmd.sunk | while | flops 6291463 | bytes 4981427 | solution.py:100
  106.5 3.1 fusion.37
  112.2 3.1 fusion.37
  117.8 3.1 fusion.37
  123.5 3.1 fusion.37
  129.2 3.1 fusion.37
  134.9 3.1 fusion.37
  140.5 3.1 fusion.37
  146.2 3.1 fusion.37
  151.9 3.1 fusion.37
  157.5 3.1 fusion.37
  163.2 3.1 fusion.37
  168.9 3.1 fusion.37
  174.6 3.1 fusion.37
  286.3 32.7 %fusion.11 = f32[32,32,1024]{2,1,0:T(8,128)} fusion(f32[32,32,2048]{2,1,0:T(8,128)} %get-tuple-element.70, f32[1024,1024]{1,0:T(8,128)} %get-tuple-element.88, f32[1024,1024]{1,0:T(8,128)} %get-tuple-element.87), kind=kOutput, calls=%fused_computation.22 | convolution fusion | flops 25771900928 | bytes 20971520 | tf_op jit(solution)/shard_map/dot_general | solution.py:101
  319.0 87.3 %reduce-scatter.2.cloned.1.call-done = f32[8,32,1024]{2,1,0:T(8,128)} async-done(((f32[32,32,1024]{2,1,0:T(8,128)}), f32[8,32,1024]{2,1,0:T(8,128)}) %reduce-scatter.2.cloned.1.call-update) | async-done | bytes 1048592 | tf_op jit(solution)/shard_map/reduce_scatter | solution.py:107
  (122 shorter events, 118.7 us)
Async XLA Ops:
  6.5 399.9 %reduce-scatter.2.cloned.1.call-start = ((), (), s32[]{:S(2)}) async-start(), calls=%async_computation.1 | async-start | bytes 5242880 | tf_op jit(solution)/shard_map/reduce_scatter | solution.py:107
  7.4 36.5 %copy-start.5 = (s32[32,4]{0,1:T(4,128)S(1)}, s32[32,4]{0,1:T(4,128)}, u32[]{:S(2)}) copy-start(s32[32,4]{0,1:T(4,128)} %param.7) | copy-start | bytes 1540
  7.4 36.5 %copy-start.6 = (s32[32,4]{0,1:T(4,128)S(1)}, s32[32,4]{0,1:T(4,128)}, u32[]{:S(2)}) copy-start(s32[32,4]{0,1:T(4,128)} %param.8) | copy-start | bytes 1540
  7.4 39.8 %copy-start.4 = (bf16[32,16384]{1,0:T(8,128)(2,1)S(1)}, bf16[32,16384]{1,0:T(8,128)(2,1)}, u32[]{:S(2)}) copy-start(bf16[32,16384]{1,0:T(8,128)(2,1)} %param.6) | copy-start | bytes 3145732
  7.4 39.8 %collective-permute-start = (bf16[32,1024]{1,0:T(8,128)(2,1)S(1)}, bf16[32,1024]{1,0:T(8,128)(2,1)S(1)}, u32[]{:S(2)}, u32[]{:S(2)}) collective-permute-start(bf16[32,1024]{1,0:T(8,128)(2,1)S(1)} %slice.39), channel_id=1, source_target_pairs={{1,0},{2,1},{3,2},{5,4},{6,5},{7,6},{9,8},{10,9},{11,10},{13,12},{... | collective-permute-start | bytes 196616 | tf_op jit(solution)/shard_map/ppermute | solution.py:18
  48.1 2.2 copy-start.3
  57.0 1.9 copy-start
  74.7 1.0 copy-start.1
  75.7 23.0 %collective-permute-start.1 = (bf16[32,16,2048]{2,1,0:T(8,128)(2,1)S(1)}, bf16[32,16,2048]{2,1,0:T(8,128)(2,1)}, u32[]{:S(2)}, u32[]{:S(2)}) collective-permute-start(bf16[32,16,2048]{2,1,0:T(8,128)(2,1)S(1)} %pad_maximum_fusion.1), channel_id=1, source_target_pairs={{0,4},{4,8},{8,12},{1,5},{5,9},{9,13},{2,6},{6,10},{10,14},{3,7},{... | collective-permute-start | bytes 6291464 | tf_op jit(solution)/shard_map/ppermute | solution.py:26
  79.4 19.3 %collective-permute-start.2 = (bf16[32,16,2048]{2,1,0:T(8,128)(2,1)S(1)}, bf16[32,16,2048]{2,1,0:T(8,128)(2,1)}, u32[]{:S(2)}, u32[]{:S(2)}) collective-permute-start(bf16[32,16,2048]{2,1,0:T(8,128)(2,1)S(1)} %pad_maximum_fusion.1), channel_id=1, source_target_pairs={{4,0},{8,4},{12,8},{5,1},{9,5},{13,9},{6,2},{10,6},{14,10},{7,3},{... | collective-permute-start | bytes 6291464 | tf_op jit(solution)/shard_map/ppermute | solution.py:29
  80.7 18.0 %copy-start.2 = (bf16[32,16,1024]{2,1,0:T(8,128)(2,1)S(1)}, bf16[32,16,1024]{2,1,0:T(8,128)(2,1)}, u32[]{:S(2)}) copy-start(bf16[32,16,1024]{2,1,0:T(8,128)(2,1)} %copy-done.1) | copy-start | bytes 3145732
  98.7 5.9 %copy-start.7 = (s32[32]{0:T(128)S(1)}, s32[32]{0:T(128)}, u32[]{:S(2)}) copy-start(s32[32]{0:T(128)} %param.9) | copy-start | bytes 388
Sparse Core Ops, SparseCore 0:
  319.2 87.1 reduce-scatter.1
where the time goes:
time: 415 us; the launch traced here: 413 us
  other arithmetic  191 us (46%)
  waiting for transfers between devices  87.4 us (21%)
  loops' own time  41.8 us (10%)
  matrix products  39.4 us (9%)
  local copies, waits for them, and re-layouts  33.6 us (8%)
  between operations  13.6 us (3%)
  starting transfers between devices  6.42 us (2%)
    reduce_sum x32, other arithmetic, one_slot(): real_sum = jnp.sum(real_own * real_far + imag_own * imag_far, axis=1)  98 us
    reduce_scatter x1, waiting for transfers between devices, shards(): lax.psum_scatter(folded.reshape(lax.axis_size('tm') * slot_rows, channels...  87.3 us
    another operation x1, loops' own time, shards(): stack = lax.map(one_slot, offsets)  41.8 us
    another operation x2, other arithmetic  38 us
    dot_general x1, matrix products, shards(): jnp.dot(stack.reshape(lax.axis_size('tm') * slot_rows * channels, NFFT),...  32.7 us
    dynamic_update_slice x32, other arithmetic, shards(): stack = lax.map(one_slot, offsets)  23.3 us
    dynamic_slice x32, local copies, waits for them, and re-layouts, shards(): stack = lax.map(one_slot, offsets)  18.6 us
    mul x1, other arithmetic, lag_table(): weight * jnp.cos(phase)  18 us
  transfers between devices with their start and end apart: 4, of which 1 were waited for; matrix products, arithmetic and copies ran while one was open for 14% of the time, Pallas kernels for 0%

commit v1 on v0

v1 whole, which is shorter than its diff:
```python
import math

import jax
import jax.numpy as jnp
import numpy as np
from jax import lax
from jax.experimental import pallas as pl
from jax.experimental.pallas import tpu as pltpu
from jax.sharding import PartitionSpec as P

NFFT = 2048
HALF = 1024
LAGS = 1024
BAND = 64
BLK = 256
LANE = 128


def transform_tables():
    rows = np.arange(HALF)[:, None]
    tabs = np.zeros((2, 2, HALF, 512), np.float32)
    for p in range(2):
        for jp in range(2):
            f = (2 * (256 * jp + np.arange(256)) + p)[None, :]
            phase = (rows * f % NFFT) * (2.0 * math.pi / NFFT)
            tabs[p, jp, :, :256] = np.cos(phase)
            tabs[p, jp, :, 256:] = -np.sin(phase)
    return tabs.astype(jnp.bfloat16)


def lag_table(segments):
    freqs = np.concatenate([np.arange(0, HALF, 2), np.arange(1, HALF, 2)])[:, None]
    shifts = np.arange(LAGS)[None, :] - LAGS // 2
    phase = (freqs * shifts % NFFT) * (2.0 * math.pi / NFFT)
    weight = np.where(freqs == 0, 1.0, 2.0) / math.sqrt(NFFT * segments)
    table = np.concatenate([weight * np.cos(phase), -weight * np.sin(phase)], axis=0)
    return table.astype(np.float32).astype(jnp.bfloat16)


def band_ones():
    place = np.arange(256) // 32
    return (place[:, None] == place[None, :]).astype(np.float32).astype(jnp.bfloat16)


def taper_row():
    n = np.arange(NFFT, dtype=np.float32)[None, :]
    return (0.5 - 0.5 * np.cos(n * np.float32(2.0 * math.pi / NFFT))).astype(np.float32)


def spectra(ext, place, taper, tabs, ones, even, odd, near, wide, diff):
    for s in range(16):
        low = ext[:, s * HALF : (s + 1) * HALF].astype(jnp.float32) * taper[:, :HALF]
        high = ext[:, (s + 1) * HALF : (s + 2) * HALF].astype(jnp.float32) * taper[:, HALF:]
        low = low.astype(jnp.bfloat16).astype(jnp.float32)
        high = high.astype(jnp.bfloat16).astype(jnp.float32)
        even[s * 32 : (s + 1) * 32, :] = (low + high).astype(jnp.bfloat16)
        odd[s * 32 : (s + 1) * 32, :] = (low - high).astype(jnp.bfloat16)

    @pl.loop(0, 4)
    def _(step):
        jp = step % 2
        part = step // 2
        rows = pl.ds(pl.multiple_of(part * 256, 256), 256)
        spec = [
            jnp.dot(half[rows, :], tabs[p, jp], preferred_element_type=jnp.float32)
            for p, half in enumerate((even, odd))
        ]
        power = sum(v[:, :256] * v[:, :256] + v[:, 256:] * v[:, 256:] for v in spec)
        total = jnp.dot(power.astype(jnp.bfloat16), ones[...], preferred_element_type=jnp.float32)
        factor = lax.rsqrt(total * (1.0 / BAND) + 1e-6)
        for p in range(2):
            c = (spec[p][:, :256] * factor).astype(jnp.bfloat16).astype(jnp.float32)
            d = (spec[p][:, 256:] * factor).astype(jnp.bfloat16).astype(jnp.float32)
            for dest, val in ((near, c), (wide, c + d), (diff, d - c)):
                for s in range(8):
                    for h in range(2):
                        dest[part * 8 + s, p * 4 + jp * 2 + h, place * 32 : (place + 1) * 32, :] = val[
                            s * 32 : (s + 1) * 32, h * LANE : (h + 1) * LANE
                        ]


def correlate(offs, first, slots, near, wide, diff, stack):
    @pl.loop(0, 32)
    def _(step):
        j = step // 4
        i = step % 4
        own = pl.ds(pl.multiple_of(32 + i * 8, 8), 8)
        far = [pl.ds(32 + i * 8 + offs[first + k], 8) for k in range(slots)]
        acc = [[None] * 3 for _ in range(slots)]
        for s in range(16):
            a = near[s, j, own, :]
            ab = wide[s, j, own, :]
            b = ab - a
            for k in range(slots):
                terms = (
                    near[s, j, far[k], :] * ab,
                    wide[s, j, far[k], :] * a,
                    diff[s, j, far[k], :] * b,
                )
                for t in range(3):
                    acc[k][t] = terms[t] if acc[k][t] is None else acc[k][t] + terms[t]
        col = pl.multiple_of(j * LANE, LANE)
        for k in range(slots):
            k1, k2, k3 = acc[k]
            rows = pl.ds(pl.multiple_of(k * 32 + i * 8, 8), 8)
            stack[rows, pl.ds(col, LANE)] = k1 + k3
            stack[rows, pl.ds(pl.multiple_of(col + HALF, LANE), LANE)] = k1 - k2


def kernel(slots, offs, low, mid, high, taper, tabs, lags, ones, out, even, odd, near, wide, diff, stack, stackb):
    for place, ext in enumerate((low, mid, high)):
        spectra(ext, place, taper, tabs, ones, even, odd, near, wide, diff)
    rows = slots * 32

    @pl.loop(0, 32 // slots)
    def _(block):
        correlate(offs, block * slots, slots, near, wide, diff, stack)
        stackb[...] = stack[...].astype(jnp.bfloat16)

        @pl.loop(0, LAGS // 256)
        def _(n):
            cols = pl.ds(pl.multiple_of(n * 256, 256), 256)
            fold = jnp.dot(stackb[...], lags[:, cols], preferred_element_type=jnp.float32)
            out[pl.ds(pl.multiple_of(block * rows, rows), rows), cols] = fold.astype(out.dtype)


def shards(samples, gap_start, gap_len, offsets, taper, tabs, lags, ones):
    channels, local_len = samples.shape
    tm_count = lax.axis_size("tm")
    chan_count = lax.axis_size("chan")
    slots = offsets.shape[0] // tm_count
    blocks = (lax.axis_index("tm") * local_len + jnp.arange(local_len, dtype=jnp.int32)) // BLK
    covered = jnp.any(
        (blocks[None, None, :] >= gap_start[:, :, None])
        & (blocks[None, None, :] < (gap_start + gap_len)[:, :, None]),
        axis=1,
    )
    masked = jnp.where(covered, jnp.zeros_like(samples), samples)
    back = [(i + 1, i) for i in range(tm_count - 1)]
    ext = jnp.concatenate([masked, lax.ppermute(masked[:, :HALF], "tm", back)], axis=1)
    forward = [(i, i + 1) for i in range(chan_count - 1)]
    low = lax.ppermute(ext, "chan", forward)
    high = lax.ppermute(ext, "chan", [(b, a) for a, b in forward])
    vmem = pl.BlockSpec(memory_space=pltpu.VMEM)
    part = pl.pallas_call(
        lambda *refs: kernel(slots, *refs),
        out_shape=jax.ShapeDtypeStruct((32 * channels, LAGS), jnp.bfloat16),
        in_specs=[pl.BlockSpec(memory_space=pltpu.SMEM)] + [vmem] * 7,
        out_specs=vmem,
        scratch_shapes=[
            pltpu.VMEM((512, HALF), jnp.bfloat16),
            pltpu.VMEM((512, HALF), jnp.bfloat16),
            pltpu.VMEM((16, 8, 96, LANE), jnp.float32),
            pltpu.VMEM((16, 8, 96, LANE), jnp.float32),
            pltpu.VMEM((16, 8, 96, LANE), jnp.float32),
            pltpu.VMEM((slots * 32, NFFT), jnp.float32),
            pltpu.VMEM((slots * 32, NFFT), jnp.bfloat16),
        ],
        compiler_params=pltpu.CompilerParams(vmem_limit_bytes=60 * 1024 * 1024),
    )(offsets, low, ext, high, taper, tabs, lags, ones)
    part = part.reshape(tm_count, slots, channels, LAGS)
    mixed = lax.all_to_all(part, "tm", split_axis=0, concat_axis=0)
    return jnp.sum(mixed.astype(jnp.float32), axis=0)


def solution(mesh):
    placed = (P(("win", "chan"), "tm"), P(("win", "chan"), None), P(("win", "chan"), None), P())
    inner = jax.shard_map(
        shards,
        mesh=mesh,
        in_specs=placed + (P(),) * 4,
        out_specs=P("tm", ("win", "chan"), None),
        check_vma=False,
    )

    def run(samples, gap_start, gap_len, offsets):
        segments = samples.shape[1] // HALF
        return inner(
            samples, gap_start, gap_len, offsets, taper_row(), transform_tables(), lag_table(segments), band_ones()
        )

    return run
```

time: 415 us -> 137 us (0.33)
  the two profiles are of different devices: /device:TPU:0 before, /device:TPU:1 now
where the time goes in v1:
time: 137 us; the launch traced here: 136 us
  Pallas kernels  61.7 us (45%)
  blocking collectives  42.1 us (31%)
  waiting for transfers between devices  16.8 us (12%)
  starting transfers between devices  8.23 us (6%)
  other arithmetic  6.37 us (5%)
    pallas_call x1, Pallas kernels, shards(): pl.pallas_call(lambda *refs: kernel(slots, *refs), out_shape=jax.ShapeDty...  61.7 us
    all_to_all x1, blocking collectives, shards(): mixed = lax.all_to_all(part, 'tm', split_axis=0, concat_axis=0)  42.1 us
    ppermute x1, waiting for transfers between devices, shards(): high = lax.ppermute(ext, 'chan', [(b, a) for a, b in forward])  11.2 us
    ppermute x1, waiting for transfers between devices, shards(): lax.ppermute(masked[:, :HALF], 'tm', back)  4.38 us
    ppermute x1, starting transfers between devices, shards(): low = lax.ppermute(ext, 'chan', forward)  3.48 us
    ppermute x1, starting transfers between devices, shards(): high = lax.ppermute(ext, 'chan', [(b, a) for a, b in forward])  3.45 us
    reduce_or x1, other arithmetic, shards(): jnp.any((blocks[None, None, :] >= gap_start[:, :, None]) & (blocks[None,...  2.85 us
  transfers between devices with their start and end apart: 3, of which 3 were waited for; matrix products, arithmetic and copies ran while one was open for 0% of the time, Pallas kernels for 0%

profile of v1, /device:TPU:1, one launch (start us, length us, event | category | flops | bytes accessed | tf_op | source)
XLA Modules:
  0.0 136.3 jit_solution(15058134134295600428)
XLA Ops:
  0.0 0.7 add.20
  0.8 2.9 %and_reduce_fusion = pred[32,16384]{1,0:T(8,128)(4,1)S(1)} fusion(s32[32,4]{0,1:T(4,128)S(1)} %add.20, s32[32,4]{0,1:T(4,128)} %param.9, s32[16384]{0:T(1024)S(1)} %add_select_fusion), kind=kLoop, calls=%fused_computation | loop fusion | flops 7864320 | bytes 590848 | tf_op jit(solution)/shard_map/reduce_or | solution.py:133
  3.6 1.3 broadcast_select_fusion
  5.0 1.3 collective-permute-start
  6.3 4.4 %collective-permute-done = bf16[32,1024]{1,0:T(8,128)(2,1)S(1)} collective-permute-done((bf16[32,1024]{1,0:T(8,128)(2,1)S(1)}, bf16[32,1024]{1,0:T(8,128)(2,1)S(1)}, u32[]{:S(2)}, u32[]{:S(2)}) %collective-permute-start) | collective-permute-done | bytes 65568 | tf_op jit(solution)/shard_map/ppermute | solution.py:140
  10.6 0.1 pad_maximum_fusion.refs_2_
  10.7 0.0 copy-start
  10.7 3.5 %collective-permute-start.2 = (bf16[32,17408]{1,0:T(8,128)(2,1)S(1)}, bf16[32,17408]{1,0:T(8,128)(2,1)S(1)}, u32[]{:S(2)}, u32[]{:S(2)}) collective-permute-start(bf16[32,17408]{1,0:T(8,128)(2,1)S(1)} %pad_maximum_fusion.refs_2_), channel_id=1, source_target_pairs={{4,0},{8,4},{12,8},{5,1},{9,5},{13,9},{6,2},{10,6},{14,10},{7,3},{... | collective-permute-start | bytes 3342344 | tf_op jit(solution)/shard_map/ppermute | solution.py:143
  14.2 3.5 %collective-permute-start.1 = (bf16[32,17408]{1,0:T(8,128)(2,1)S(1)}, bf16[32,17408]{1,0:T(8,128)(2,1)S(1)}, u32[]{:S(2)}, u32[]{:S(2)}) collective-permute-start(bf16[32,17408]{1,0:T(8,128)(2,1)S(1)} %pad_maximum_fusion.refs_2_), channel_id=1, source_target_pairs={{0,4},{4,8},{8,12},{1,5},{5,9},{9,13},{2,6},{6,10},{10,14},{3,7},{... | collective-permute-start | bytes 3342344 | tf_op jit(solution)/shard_map/ppermute | solution.py:142
  17.7 11.2 %collective-permute-done.2.refs_3_ = bf16[32,17408]{1,0:T(8,128)(2,1)S(1)} collective-permute-done((bf16[32,17408]{1,0:T(8,128)(2,1)S(1)}, bf16[32,17408]{1,0:T(8,128)(2,1)S(1)}, u32[]{:S(2)}, u32[]{:S(2)}) %collective-permute-start.2) | collective-permute-done | bytes 1114144 | tf_op jit(solution)/shard_map/ppermute | solution.py:143
  28.9 0.0 copy-start.1
  28.9 1.2 collective-permute-done.1.refs_1_
  30.1 0.0 copy-done
  30.1 0.0 copy-done.1
  30.1 0.0 copy-start.2
  30.1 1.0 copy-done.2
  31.1 61.7 %shard_map.82 = bf16[1024,1024]{1,0:T(8,128)(2,1)} custom-call(s32[32]{0:T(128)} %refs_0_.1, bf16[32,17408]{1,0:T(8,128)(2,1)} %copy-done.2, bf16[32,17408]{1,0:T(8,128)(2,1)} %copy-done, bf16[32,17408]{1,0:T(8,128)(2,1)} %copy-done.1, f32[1,2048]{1,0:T(1,128)} %constant.36.clone.refs_4_, bf16[2,2,1024,512]{3,2,1,0:T(8,128)(2,1)} %constant.37.clone.refs_5_, ...), custom_call_target="tpu_custom_call" | custom-call | tf_op jit(solution)/shard_map/pallas_call | solution.py:145
  92.8 42.1 %all_to_all.5 = bf16[4,8,32,1024]{3,2,1,0:T(8,128)(2,1)S(1)} all-to-all(bf16[4,8,32,1024]{3,2,1,0:T(8,128)(2,1)} %bitcast.1), channel_id=1, replica_groups=mesh['win'=2,'chan'=4,'tm'=4] {'tm'}, dimensions={0} | all-to-all | bytes 4194304 | tf_op jit(solution)/shard_map/all_to_all | solution.py:162
  134.9 1.4 %convert_reduce_fusion = f32[8,32,1024]{2,1,0:T(8,128)} fusion(bf16[4,8,32,1024]{3,2,1,0:T(8,128)(2,1)S(1)} %all_to_all.5), kind=kLoop, calls=%fused_computation.1 | loop fusion | flops 1835008 | bytes 3145728 | tf_op jit(solution)/shard_map/reduce_sum | solution.py:163
  (2 shorter events, 0.1 us)
Async XLA Ops:
  5.0 5.7 %collective-permute-start = (bf16[32,1024]{1,0:T(8,128)(2,1)S(1)}, bf16[32,1024]{1,0:T(8,128)(2,1)S(1)}, u32[]{:S(2)}, u32[]{:S(2)}) collective-permute-start(bf16[32,1024]{1,0:T(8,128)(2,1)S(1)} %slice.4), channel_id=1, source_target_pairs={{1,0},{2,1},{3,2},{5,4},{6,5},{7,6},{9,8},{10,9},{11,10},{13,12},{... | collective-permute-start | bytes 196616 | tf_op jit(solution)/shard_map/ppermute | solution.py:140
  10.7 19.4 %copy-start = (bf16[32,17408]{1,0:T(8,128)(2,1)}, bf16[32,17408]{1,0:T(8,128)(2,1)S(1)}, u32[]{:S(2)}) copy-start(bf16[32,17408]{1,0:T(8,128)(2,1)S(1)} %pad_maximum_fusion.refs_2_) | copy-start | bytes 3342340
  10.7 18.2 %collective-permute-start.2 = (bf16[32,17408]{1,0:T(8,128)(2,1)S(1)}, bf16[32,17408]{1,0:T(8,128)(2,1)S(1)}, u32[]{:S(2)}, u32[]{:S(2)}) collective-permute-start(bf16[32,17408]{1,0:T(8,128)(2,1)S(1)} %pad_maximum_fusion.refs_2_), channel_id=1, source_target_pairs={{4,0},{8,4},{12,8},{5,1},{9,5},{13,9},{6,2},{10,6},{14,10},{7,3},{... | collective-permute-start | bytes 3342344 | tf_op jit(solution)/shard_map/ppermute | solution.py:143
  14.2 15.9 %collective-permute-start.1 = (bf16[32,17408]{1,0:T(8,128)(2,1)S(1)}, bf16[32,17408]{1,0:T(8,128)(2,1)S(1)}, u32[]{:S(2)}, u32[]{:S(2)}) collective-permute-start(bf16[32,17408]{1,0:T(8,128)(2,1)S(1)} %pad_maximum_fusion.refs_2_), channel_id=1, source_target_pairs={{0,4},{4,8},{8,12},{1,5},{5,9},{9,13},{2,6},{6,10},{10,14},{3,7},{... | collective-permute-start | bytes 3342344 | tf_op jit(solution)/shard_map/ppermute | solution.py:142
  28.9 1.2 copy-start.1
  30.1 1.0 copy-start.2

commit v2 on v1

--- a/solution.py
+++ b/solution.py
@@ -48,13 +48,18 @@
 
 
 def spectra(ext, place, taper, tabs, ones, even, odd, near, wide, diff):
-    for s in range(16):
-        low = ext[:, s * HALF : (s + 1) * HALF].astype(jnp.float32) * taper[:, :HALF]
-        high = ext[:, (s + 1) * HALF : (s + 2) * HALF].astype(jnp.float32) * taper[:, HALF:]
+    @pl.loop(0, 16)
+    def _(s):
+        begin = pl.multiple_of(s * HALF, HALF)
+        low = ext[place, :, pl.ds(begin, HALF)].astype(jnp.float32) * taper[:, :HALF]
+        high = ext[place, :, pl.ds(pl.multiple_of(begin + HALF, HALF), HALF)].astype(jnp.float32) * taper[:, HALF:]
         low = low.astype(jnp.bfloat16).astype(jnp.float32)
         high = high.astype(jnp.bfloat16).astype(jnp.float32)
-        even[s * 32 : (s + 1) * 32, :] = (low + high).astype(jnp.bfloat16)
-        odd[s * 32 : (s + 1) * 32, :] = (low - high).astype(jnp.bfloat16)
+        rows = pl.ds(pl.multiple_of(s * 32, 32), 32)
+        even[rows, :] = (low + high).astype(jnp.bfloat16)
+        odd[rows, :] = (low - high).astype(jnp.bfloat16)
+
+    place_rows = pl.ds(pl.multiple_of(place * 32, 32), 32)
 
     @pl.loop(0, 4)
     def _(step):
@@ -74,7 +79,7 @@
             for dest, val in ((near, c), (wide, c + d), (diff, d - c)):
                 for s in range(8):
                     for h in range(2):
-                        dest[part * 8 + s, p * 4 + jp * 2 + h, place * 32 : (place + 1) * 32, :] = val[
+                        dest[part * 8 + s, p * 4 + jp * 2 + h, place_rows, :] = val[
                             s * 32 : (s + 1) * 32, h * LANE : (h + 1) * LANE
                         ]
 
@@ -107,60 +112,205 @@
             stack[rows, pl.ds(pl.multiple_of(col + HALF, LANE), LANE)] = k1 - k2
 
 
-def kernel(slots, offs, low, mid, high, taper, tabs, lags, ones, out, even, odd, near, wide, diff, stack, stackb):
-    for place, ext in enumerate((low, mid, high)):
+MESH = pl.DeviceIdType.MESH
+
+
+def kernel(
+    slots, ranges, offs, starts, lens, x, taper, tabs, lags, ones, out,
+    ext, even, odd, near, wide, diff, stack, stackb, sent, got,
+    halo_send, halo_recv, sum_send, sum_recv,
+):
+    me, z = lax.axis_index("chan"), lax.axis_index("tm")
+    win = lax.axis_index("win")
+    chans = lax.axis_size("chan")
+    local = x.shape[1]
+    rows = slots * 32
+    lower, upper = me > 0, me < chans - 1
+    early, late = z > 0, z < ranges - 1
+
+    barrier = pltpu.get_barrier_semaphore()
+    for r in range(1, ranges):
+        pl.semaphore_signal(
+            barrier, inc=1, device_id=(win, me, lax.rem(z + r, ranges)), device_id_type=MESH
+        )
+    for side, there in ((-1, lower), (1, upper)):
+        for dz, ahead in ((-1, early), (0, True), (1, late)):
+            @pl.when(jnp.logical_and(there, ahead))
+            def _(side=side, dz=dz):
+                pl.semaphore_signal(
+                    barrier, inc=1, device_id=(win, me + side, z + dz), device_id_type=MESH
+                )
+
+    @pl.loop(0, local // HALF)
+    def _(s):
+        begin = pl.multiple_of(s * HALF, HALF)
+        for q in range(HALF // BLK):
+            block = z * (local // BLK) + s * (HALF // BLK) + q
+            cols = pl.ds(pl.multiple_of(begin + q * BLK, BLK), BLK)
+            hit = (starts[...] <= block) & (block < starts[...] + lens[...])
+            count = jnp.sum(hit.astype(jnp.float32), axis=1, keepdims=True)
+            value = x[:, cols].astype(jnp.float32)
+            ext[1, :, cols] = jnp.where(count > 0.0, 0.0, value).astype(jnp.bfloat16)
+
+    edge = pl.ds(local, HALF)
+
+    @pl.when(jnp.logical_not(late))
+    def _():
+        for p in range(3):
+            ext[p, :, edge] = jnp.zeros((32, HALF), jnp.bfloat16)
+
+    for p, there in ((0, lower), (2, upper)):
+        @pl.when(jnp.logical_not(there))
+        def _(p=p):
+            @pl.loop(0, local // HALF)
+            def _(s):
+                ext[p, :, pl.ds(pl.multiple_of(s * HALF, HALF), HALF)] = jnp.zeros((32, HALF), jnp.bfloat16)
+
+            @pl.when(late)
+            def _():
+                ext[p, :, edge] = jnp.zeros((32, HALF), jnp.bfloat16)
+
+    sides = lower.astype(jnp.int32) + upper.astype(jnp.int32)
+    around = 1 + early.astype(jnp.int32) + late.astype(jnp.int32)
+    pl.semaphore_wait(barrier, ranges - 1 + sides * around)
+
+    def body_copy(p, side):
+        return pltpu.make_async_remote_copy(
+            src_ref=ext.at[1, :, pl.ds(0, local)], dst_ref=ext.at[p, :, pl.ds(0, local)],
+            send_sem=halo_send.at[2 * p], recv_sem=halo_recv.at[2 * p],
+            device_id=(win, me + side, z), device_id_type=MESH,
+        )
+
+    def head_copy(p, side):
+        return pltpu.make_async_remote_copy(
+            src_ref=ext.at[1, :, pl.ds(0, HALF)], dst_ref=ext.at[p, :, edge],
+            send_sem=halo_send.at[2 * p + 1], recv_sem=halo_recv.at[2 * p + 1],
+            device_id=(win, me + side, z - 1), device_id_type=MESH,
+        )
+
+    @pl.when(early)
+    def _():
+        head_copy(1, 0).start()
+
+    for p, side, there in ((0, 1, upper), (2, -1, lower)):
+        @pl.when(there)
+        def _(p=p, side=side):
+            @pl.when(early)
+            def _():
+                head_copy(p, side).start()
+
+            body_copy(p, side).start()
+
+    @pl.loop(0, 3)
+    def _(q):
+        first = jnp.where(me % 2 == 0, 2, 0)
+        place = jnp.where(q == 0, 1, jnp.where(q == 1, first, 2 - first))
+
+        for p, there in ((0, lower), (1, None), (2, upper)):
+            present = place == p if there is None else jnp.logical_and(place == p, there)
+
+            @pl.when(present)
+            def _(p=p):
+                if p != 1:
+                    body_copy(p, 0).wait_recv()
+
+                @pl.when(late)
+                def _():
+                    head_copy(p, 0).wait_recv()
+
         spectra(ext, place, taper, tabs, ones, even, odd, near, wide, diff)
-    rows = slots * 32
-
-    @pl.loop(0, 32 // slots)
-    def _(block):
-        correlate(offs, block * slots, slots, near, wide, diff, stack)
+
+    def sum_copy(r):
+        return pltpu.make_async_remote_copy(
+            src_ref=sent.at[r - 1], dst_ref=got.at[r - 1],
+            send_sem=sum_send.at[r - 1], recv_sem=sum_recv.at[r - 1],
+            device_id=(win, me, lax.rem(z + r, ranges)), device_id_type=MESH,
+        )
+
+    @pl.loop(0, ranges)
+    def _(t):
+        r = ranges - 1 - t
+        target = lax.rem(z + r, ranges)
+        correlate(offs, target * slots, slots, near, wide, diff, stack)
         stackb[...] = stack[...].astype(jnp.bfloat16)
 
         @pl.loop(0, LAGS // 256)
         def _(n):
             cols = pl.ds(pl.multiple_of(n * 256, 256), 256)
             fold = jnp.dot(stackb[...], lags[:, cols], preferred_element_type=jnp.float32)
-            out[pl.ds(pl.multiple_of(block * rows, rows), rows), cols] = fold.astype(out.dtype)
+
+            @pl.when(r > 0)
+            def _():
+                sent[r - 1, :, cols] = fold.astype(jnp.bfloat16)
+
+            @pl.when(r == 0)
+            def _():
+                out[:, cols] = fold
+
+        @pl.when(r > 0)
+        def _():
+            sum_copy(r).start()
+
+    @pl.loop(0, ranges - 1)
+    def _(t):
+        r = ranges - 1 - t
+        sum_copy(r).wait_recv()
+
+        @pl.loop(0, rows // 32)
+        def _(n):
+            part = pl.ds(pl.multiple_of(n * 32, 32), 32)
+            out[part, :] = out[part, :] + got[r - 1, part, :].astype(jnp.float32)
+
+    @pl.loop(0, ranges - 1)
+    def _(t):
+        sum_copy(ranges - 1 - t).wait_send()
+
+    @pl.when(early)
+    def _():
+        head_copy(1, 0).wait_send()
+
+    for p, side, there in ((0, 1, upper), (2, -1, lower)):
+        @pl.when(there)
+        def _(p=p, side=side):
+            @pl.when(early)
+            def _():
+                head_copy(p, side).wait_send()
+
+            body_copy(p, side).wait_send()
 
 
 def shards(samples, gap_start, gap_len, offsets, taper, tabs, lags, ones):
     channels, local_len = samples.shape
-    tm_count = lax.axis_size("tm")
-    chan_count = lax.axis_size("chan")
-    slots = offsets.shape[0] // tm_count
-    blocks = (lax.axis_index("tm") * local_len + jnp.arange(local_len, dtype=jnp.int32)) // BLK
-    covered = jnp.any(
-        (blocks[None, None, :] >= gap_start[:, :, None])
-        & (blocks[None, None, :] < (gap_start + gap_len)[:, :, None]),
-        axis=1,
-    )
-    masked = jnp.where(covered, jnp.zeros_like(samples), samples)
-    back = [(i + 1, i) for i in range(tm_count - 1)]
-    ext = jnp.concatenate([masked, lax.ppermute(masked[:, :HALF], "tm", back)], axis=1)
-    forward = [(i, i + 1) for i in range(chan_count - 1)]
-    low = lax.ppermute(ext, "chan", forward)
-    high = lax.ppermute(ext, "chan", [(b, a) for a, b in forward])
+    ranges = lax.axis_size("tm")
+    slots = offsets.shape[0] // ranges
+    rows = slots * channels
     vmem = pl.BlockSpec(memory_space=pltpu.VMEM)
     part = pl.pallas_call(
-        lambda *refs: kernel(slots, *refs),
-        out_shape=jax.ShapeDtypeStruct((32 * channels, LAGS), jnp.bfloat16),
+        lambda *refs: kernel(slots, ranges, *refs),
+        out_shape=jax.ShapeDtypeStruct((rows, LAGS), jnp.float32),
         in_specs=[pl.BlockSpec(memory_space=pltpu.SMEM)] + [vmem] * 7,
         out_specs=vmem,
         scratch_shapes=[
+            pltpu.VMEM((3, channels, local_len + HALF), jnp.bfloat16),
             pltpu.VMEM((512, HALF), jnp.bfloat16),
             pltpu.VMEM((512, HALF), jnp.bfloat16),
             pltpu.VMEM((16, 8, 96, LANE), jnp.float32),
             pltpu.VMEM((16, 8, 96, LANE), jnp.float32),
             pltpu.VMEM((16, 8, 96, LANE), jnp.float32),
-            pltpu.VMEM((slots * 32, NFFT), jnp.float32),
-            pltpu.VMEM((slots * 32, NFFT), jnp.bfloat16),
+            pltpu.VMEM((rows, NFFT), jnp.float32),
+            pltpu.VMEM((rows, NFFT), jnp.bfloat16),
+            pltpu.VMEM((ranges - 1, rows, LAGS), jnp.bfloat16),
+            pltpu.VMEM((ranges - 1, rows, LAGS), jnp.bfloat16),
+            pltpu.SemaphoreType.DMA((6,)),
+            pltpu.SemaphoreType.DMA((6,)),
+            pltpu.SemaphoreType.DMA((ranges - 1,)),
+            pltpu.SemaphoreType.DMA((ranges - 1,)),
         ],
-        compiler_params=pltpu.CompilerParams(vmem_limit_bytes=60 * 1024 * 1024),
-    )(offsets, low, ext, high, taper, tabs, lags, ones)
-    part = part.reshape(tm_count, slots, channels, LAGS)
-    mixed = lax.all_to_all(part, "tm", split_axis=0, concat_axis=0)
-    return jnp.sum(mixed.astype(jnp.float32), axis=0)
+        compiler_params=pltpu.CompilerParams(
+            vmem_limit_bytes=60 * 1024 * 1024, collective_id=0, has_side_effects=True
+        ),
+    )(offsets, gap_start, gap_len, samples, taper, tabs, lags, ones)
+    return part.reshape(slots, channels, LAGS)
 
 
 def solution(mesh):

time: 137 us -> 91.9 us (0.67)
  the two profiles are of different devices: /device:TPU:1 before, /device:TPU:0 now
where the time goes in v2:
time: 91.9 us; the launch traced here: 91.8 us
  Pallas kernels  86.7 us (94%)
  local copies, waits for them, and re-layouts  5.03 us (5%)
    pallas_call x1, Pallas kernels, shards(): pl.pallas_call(lambda *refs: kernel(slots, ranges, *refs), out_shape=jax....  86.7 us
    unnamed x3, local copies, waits for them, and re-layouts  5.03 us

profile of v2, /device:TPU:0, one launch (start us, length us, event | category | flops | bytes accessed | tf_op | source)
XLA Modules:
  0.0 91.8 jit_solution(11001220228988228082)
XLA Ops:
  0.0 1.4 %copy.9.refs_1_ = s32[32,4]{1,0:T(8,128)} copy(s32[32,4]{0,1:T(4,128)} %param.9) | data formatting | bytes 1024 | tf_op args[1]
  1.4 1.4 %copy.10.refs_2_ = s32[32,4]{1,0:T(8,128)} copy(s32[32,4]{0,1:T(4,128)} %param.10) | data formatting | bytes 1024 | tf_op args[2]
  2.7 86.7 %shard_map.82 = f32[256,1024]{1,0:T(8,128)} custom-call(s32[32]{0:T(128)} %refs_0_.1, s32[32,4]{1,0:T(8,128)} %copy.9.refs_1_, s32[32,4]{1,0:T(8,128)} %copy.10.refs_2_, bf16[32,16384]{1,0:T(8,128)(2,1)} %refs_3_.1, f32[1,2048]{1,0:T(1,128)} %constant.8.clone.refs_4_, bf16[2,2,1024,512]{3,2,1,0:T(8,128)(2,1)} %constant.9.clone.refs_5_, ...), custom_call_target="tpu_custom_call" | custom-call | tf_op jit(solution)/shard_map/pallas_call | solution.py:288
  89.4 2.3 %copy.12 = f32[8,32,1024]{2,1,0:T(8,128)} copy(f32[8,32,1024]{2,1,0:T(8,128)} %bitcast.1) | data formatting | bytes 2097152

commit v3 on v2

--- a/solution.py
+++ b/solution.py
@@ -116,9 +116,9 @@
 
 
 def kernel(
-    slots, ranges, offs, starts, lens, x, taper, tabs, lags, ones, out,
-    ext, even, odd, near, wide, diff, stack, stackb, sent, got,
-    halo_send, halo_recv, sum_send, sum_recv,
+    slots, ranges, offs, starts, lens, x, taper, tabs_hbm, lags_hbm, ones, out,
+    tabs, lags, ext, even, odd, near, wide, diff, stack, stackb, sent, got,
+    table_sem, halo_send, halo_recv, sum_send, sum_recv,
 ):
     me, z = lax.axis_index("chan"), lax.axis_index("tm")
     win = lax.axis_index("win")
@@ -128,26 +128,43 @@
     lower, upper = me > 0, me < chans - 1
     early, late = z > 0, z < ranges - 1
 
+    load_tabs = pltpu.make_async_copy(tabs_hbm, tabs, table_sem.at[0])
+    load_lags = pltpu.make_async_copy(lags_hbm, lags, table_sem.at[1])
+    load_tabs.start()
+    load_lags.start()
     barrier = pltpu.get_barrier_semaphore()
-    for r in range(1, ranges):
-        pl.semaphore_signal(
-            barrier, inc=1, device_id=(win, me, lax.rem(z + r, ranges)), device_id_type=MESH
-        )
-    for side, there in ((-1, lower), (1, upper)):
+    for side, there in ((-1, lower), (0, True), (1, upper)):
         for dz, ahead in ((-1, early), (0, True), (1, late)):
+            if side == 0 and dz == 0:
+                continue
+
             @pl.when(jnp.logical_and(there, ahead))
             def _(side=side, dz=dz):
                 pl.semaphore_signal(
                     barrier, inc=1, device_id=(win, me + side, z + dz), device_id_type=MESH
                 )
 
+    square = (32, 32)
+    eye = (
+        lax.broadcasted_iota(jnp.int32, square, 0) == lax.broadcasted_iota(jnp.int32, square, 1)
+    ).astype(jnp.float32)
+
+    def upright(value):
+        return lax.dot_general(
+            eye, value.astype(jnp.float32), (((1,), (1,)), ((), ())),
+            precision=lax.Precision.HIGHEST, preferred_element_type=jnp.float32,
+        )
+
+    begins = upright(starts[...])
+    ends = upright(starts[...] + lens[...])
+
     @pl.loop(0, local // HALF)
     def _(s):
         begin = pl.multiple_of(s * HALF, HALF)
         for q in range(HALF // BLK):
-            block = z * (local // BLK) + s * (HALF // BLK) + q
+            block = (z * (local // BLK) + s * (HALF // BLK) + q).astype(jnp.float32)
             cols = pl.ds(pl.multiple_of(begin + q * BLK, BLK), BLK)
-            hit = (starts[...] <= block) & (block < starts[...] + lens[...])
+            hit = (begins <= block) & (block < ends)
             count = jnp.sum(hit.astype(jnp.float32), axis=1, keepdims=True)
             value = x[:, cols].astype(jnp.float32)
             ext[1, :, cols] = jnp.where(count > 0.0, 0.0, value).astype(jnp.bfloat16)
@@ -172,7 +189,7 @@
 
     sides = lower.astype(jnp.int32) + upper.astype(jnp.int32)
     around = 1 + early.astype(jnp.int32) + late.astype(jnp.int32)
-    pl.semaphore_wait(barrier, ranges - 1 + sides * around)
+    pl.semaphore_wait(barrier, (1 + sides) * around - 1)
 
     def body_copy(p, side):
         return pltpu.make_async_remote_copy(
@@ -201,6 +218,8 @@
 
             body_copy(p, side).start()
 
+    load_tabs.wait()
+
     @pl.loop(0, 3)
     def _(q):
         first = jnp.where(me % 2 == 0, 2, 0)
@@ -220,50 +239,107 @@
 
         spectra(ext, place, taper, tabs, ones, even, odd, near, wide, diff)
 
-    def sum_copy(r):
+    above, below = ranges - 1 - z, z
+    most, least = jnp.maximum(above, below), jnp.minimum(above, below)
+    far_side = jnp.where(above >= below, 1, -1)
+
+    def target_of(t):
+        u = jnp.maximum(t - (most - least), 0)
+        alone = t < most - least
+        away = jnp.where(alone, most - t, least - u // 2)
+        side = jnp.where(jnp.logical_or(alone, u % 2 == 0), far_side, -far_side)
+        return z + side * away
+
+    def pass_copy(t, target):
+        step = jnp.where(target > z, 1, -1)
+        slot = jnp.where(jnp.logical_and(step < 0, target == z + step), ranges, target)
         return pltpu.make_async_remote_copy(
-            src_ref=sent.at[r - 1], dst_ref=got.at[r - 1],
-            send_sem=sum_send.at[r - 1], recv_sem=sum_recv.at[r - 1],
-            device_id=(win, me, lax.rem(z + r, ranges)), device_id_type=MESH,
-        )
+            src_ref=sent.at[t], dst_ref=got.at[slot],
+            send_sem=sum_send.at[t], recv_sem=sum_recv.at[slot],
+            device_id=(win, me, z + step), device_id_type=MESH,
+        )
+
+    def arrival(slot):
+        return pltpu.make_async_remote_copy(
+            src_ref=sent.at[0], dst_ref=got.at[slot],
+            send_sem=sum_send.at[0], recv_sem=sum_recv.at[slot],
+            device_id=(win, me, z), device_id_type=MESH,
+        )
+
+    def origin(target):
+        return jnp.logical_or(
+            jnp.logical_and(target > z, z == 0), jnp.logical_and(target < z, z == ranges - 1)
+        )
+
+    def forward(t):
+        target = target_of(t)
+
+        @pl.when(jnp.logical_not(origin(target)))
+        def _():
+            arrival(target).wait_recv()
+
+            @pl.loop(0, rows // 32)
+            def _(n):
+                part = pl.ds(pl.multiple_of(n * 32, 32), 32)
+                total = sent[t, part, :].astype(jnp.float32) + got[target, part, :].astype(jnp.float32)
+                sent[t, part, :] = total.astype(jnp.bfloat16)
+
+            pass_copy(t, target).start()
 
     @pl.loop(0, ranges)
     def _(t):
-        r = ranges - 1 - t
-        target = lax.rem(z + r, ranges)
+        target = target_of(t)
+        last = t == ranges - 1
         correlate(offs, target * slots, slots, near, wide, diff, stack)
         stackb[...] = stack[...].astype(jnp.bfloat16)
+
+        @pl.when(t == 0)
+        def _():
+            load_lags.wait()
 
         @pl.loop(0, LAGS // 256)
         def _(n):
             cols = pl.ds(pl.multiple_of(n * 256, 256), 256)
             fold = jnp.dot(stackb[...], lags[:, cols], preferred_element_type=jnp.float32)
 
-            @pl.when(r > 0)
+            @pl.when(jnp.logical_not(last))
             def _():
-                sent[r - 1, :, cols] = fold.astype(jnp.bfloat16)
-
-            @pl.when(r == 0)
+                sent[t, :, cols] = fold.astype(jnp.bfloat16)
+
+            @pl.when(last)
             def _():
                 out[:, cols] = fold
 
-        @pl.when(r > 0)
+        @pl.when(jnp.logical_and(jnp.logical_not(last), origin(target)))
         def _():
-            sum_copy(r).start()
-
-    @pl.loop(0, ranges - 1)
-    def _(t):
-        r = ranges - 1 - t
-        sum_copy(r).wait_recv()
+            pass_copy(t, target).start()
+
+        @pl.when(jnp.logical_and(t >= 2, jnp.logical_not(last)))
+        def _():
+            forward(t - 2)
+
+    for t in range(max(ranges - 3, 0), ranges - 1):
+        forward(t)
+
+    def finish(slot):
+        arrival(slot).wait_recv()
 
         @pl.loop(0, rows // 32)
         def _(n):
             part = pl.ds(pl.multiple_of(n * 32, 32), 32)
-            out[part, :] = out[part, :] + got[r - 1, part, :].astype(jnp.float32)
+            out[part, :] = out[part, :] + got[slot, part, :].astype(jnp.float32)
+
+    @pl.when(early)
+    def _():
+        finish(z)
+
+    @pl.when(late)
+    def _():
+        finish(ranges)
 
     @pl.loop(0, ranges - 1)
     def _(t):
-        sum_copy(ranges - 1 - t).wait_send()
+        pass_copy(t, target_of(t)).wait_send()
 
     @pl.when(early)
     def _():
@@ -285,12 +361,15 @@
     slots = offsets.shape[0] // ranges
     rows = slots * channels
     vmem = pl.BlockSpec(memory_space=pltpu.VMEM)
+    hbm = pl.BlockSpec(memory_space=pl.ANY)
     part = pl.pallas_call(
         lambda *refs: kernel(slots, ranges, *refs),
         out_shape=jax.ShapeDtypeStruct((rows, LAGS), jnp.float32),
-        in_specs=[pl.BlockSpec(memory_space=pltpu.SMEM)] + [vmem] * 7,
+        in_specs=[pl.BlockSpec(memory_space=pltpu.SMEM)] + [vmem] * 4 + [hbm] * 2 + [vmem],
         out_specs=vmem,
         scratch_shapes=[
+            pltpu.VMEM(tabs.shape, jnp.bfloat16),
+            pltpu.VMEM(lags.shape, jnp.bfloat16),
             pltpu.VMEM((3, channels, local_len + HALF), jnp.bfloat16),
             pltpu.VMEM((512, HALF), jnp.bfloat16),
             pltpu.VMEM((512, HALF), jnp.bfloat16),
@@ -300,16 +379,17 @@
             pltpu.VMEM((rows, NFFT), jnp.float32),
             pltpu.VMEM((rows, NFFT), jnp.bfloat16),
             pltpu.VMEM((ranges - 1, rows, LAGS), jnp.bfloat16),
-            pltpu.VMEM((ranges - 1, rows, LAGS), jnp.bfloat16),
+            pltpu.VMEM((ranges + 1, rows, LAGS), jnp.bfloat16),
+            pltpu.SemaphoreType.DMA((2,)),
             pltpu.SemaphoreType.DMA((6,)),
             pltpu.SemaphoreType.DMA((6,)),
             pltpu.SemaphoreType.DMA((ranges - 1,)),
-            pltpu.SemaphoreType.DMA((ranges - 1,)),
+            pltpu.SemaphoreType.DMA((ranges + 1,)),
         ],
         compiler_params=pltpu.CompilerParams(
             vmem_limit_bytes=60 * 1024 * 1024, collective_id=0, has_side_effects=True
         ),
-    )(offsets, gap_start, gap_len, samples, taper, tabs, lags, ones)
+    )(offsets, gap_start.T, gap_len.T, samples, taper, tabs, lags, ones)
     return part.reshape(slots, channels, LAGS)
 
 

time: 91.9 us -> 87.3 us (0.950)
  local copies, waits for them, and re-layouts: 5.03 us -> 2.31 us
  Pallas kernels: 86.7 us -> 84.9 us
    unnamed x3 -> x1, local copies, waits for them, and re-layouts: 5.03 us -> 2.31 us
    pallas_call x1, Pallas kernels: 86.7 us -> 84.9 us  [shards(): pl.pallas_call(lambda *refs: kernel(slots, ranges, *refs), out_shape=jax....]
where the time goes in v3:
time: 87.3 us; the launch traced here: 87.2 us
  Pallas kernels  84.9 us (97%)
  local copies, waits for them, and re-layouts  2.31 us (3%)
    pallas_call x1, Pallas kernels, shards(): pl.pallas_call(lambda *refs: kernel(slots, ranges, *refs), out_shape=jax....  84.9 us
    unnamed x1, local copies, waits for them, and re-layouts  2.31 us

profile of v3, /device:TPU:0, one launch (start us, length us, event | category | flops | bytes accessed | tf_op | source)
XLA Modules:
  0.0 87.2 jit_solution(11980679461017732058)
XLA Ops:
  0.0 84.9 %shard_map.82 = f32[256,1024]{1,0:T(8,128)} custom-call(s32[32]{0:T(128)} %refs_0_.1, s32[4,32]{1,0:T(4,128)} %bitcast.4, s32[4,32]{1,0:T(4,128)} %bitcast.5, bf16[32,16384]{1,0:T(8,128)(2,1)} %refs_3_.1, f32[1,2048]{1,0:T(1,128)} %constant.8.clone.refs_4_, bf16[2,2,1024,512]{3,2,1,0:T(8,128)(2,1)} %constant.9.clone.refs_5_, ...), custom_call_target="tpu_custom_call" | custom-call | tf_op jit(solution)/shard_map/pallas_call | solution.py:365
  84.9 2.3 %copy.10 = f32[8,32,1024]{2,1,0:T(8,128)} copy(f32[8,32,1024]{2,1,0:T(8,128)} %bitcast.3) | data formatting | bytes 2097152

commit v4 on v3

--- a/solution.py
+++ b/solution.py
@@ -14,6 +14,7 @@
 BAND = 64
 BLK = 256
 LANE = 128
+PITCH = 392
 
 
 def transform_tables():
@@ -47,7 +48,7 @@
     return (0.5 - 0.5 * np.cos(n * np.float32(2.0 * math.pi / NFFT))).astype(np.float32)
 
 
-def spectra(ext, place, taper, tabs, ones, even, odd, near, wide, diff):
+def spectra(ext, place, taper, tabs, ones, even, odd, far):
     @pl.loop(0, 16)
     def _(s):
         begin = pl.multiple_of(s * HALF, HALF)
@@ -58,8 +59,6 @@
         rows = pl.ds(pl.multiple_of(s * 32, 32), 32)
         even[rows, :] = (low + high).astype(jnp.bfloat16)
         odd[rows, :] = (low - high).astype(jnp.bfloat16)
-
-    place_rows = pl.ds(pl.multiple_of(place * 32, 32), 32)
 
     @pl.loop(0, 4)
     def _(step):
@@ -76,40 +75,38 @@
         for p in range(2):
             c = (spec[p][:, :256] * factor).astype(jnp.bfloat16).astype(jnp.float32)
             d = (spec[p][:, 256:] * factor).astype(jnp.bfloat16).astype(jnp.float32)
-            for dest, val in ((near, c), (wide, c + d), (diff, d - c)):
+            for t, val in enumerate((c, c + d, d - c)):
                 for s in range(8):
                     for h in range(2):
-                        dest[part * 8 + s, p * 4 + jp * 2 + h, place_rows, :] = val[
-                            s * 32 : (s + 1) * 32, h * LANE : (h + 1) * LANE
-                        ]
-
-
-def correlate(offs, first, slots, near, wide, diff, stack):
+                        for g in range(4):
+                            row = (place * 32 + g * 8) * PITCH + (part * 8 + s) * 24 + t * 8 + p * 4 + jp * 2 + h
+                            far[pl.ds(row, 8, stride=PITCH), :] = val[
+                                s * 32 + g * 8 : s * 32 + g * 8 + 8, h * LANE : (h + 1) * LANE
+                            ]
+
+
+def correlate(offs, first, slots, far, stack, pitch):
     @pl.loop(0, 32)
-    def _(step):
-        j = step // 4
-        i = step % 4
-        own = pl.ds(pl.multiple_of(32 + i * 8, 8), 8)
-        far = [pl.ds(32 + i * 8 + offs[first + k], 8) for k in range(slots)]
+    def _(c):
+        own = pl.multiple_of((32 + c) * PITCH, 8)
+        base = [(32 + c + offs[first + k]) * PITCH for k in range(slots)]
         acc = [[None] * 3 for _ in range(slots)]
         for s in range(16):
-            a = near[s, j, own, :]
-            ab = wide[s, j, own, :]
+            a = far[pl.ds(own + s * 24, 8), :]
+            ab = far[pl.ds(own + s * 24 + 8, 8), :]
             b = ab - a
             for k in range(slots):
                 terms = (
-                    near[s, j, far[k], :] * ab,
-                    wide[s, j, far[k], :] * a,
-                    diff[s, j, far[k], :] * b,
+                    far[pl.ds(base[k] + s * 24, 8), :] * ab,
+                    far[pl.ds(base[k] + s * 24 + 8, 8), :] * a,
+                    far[pl.ds(base[k] + s * 24 + 16, 8), :] * b,
                 )
                 for t in range(3):
                     acc[k][t] = terms[t] if acc[k][t] is None else acc[k][t] + terms[t]
-        col = pl.multiple_of(j * LANE, LANE)
         for k in range(slots):
             k1, k2, k3 = acc[k]
-            rows = pl.ds(pl.multiple_of(k * 32 + i * 8, 8), 8)
-            stack[rows, pl.ds(col, LANE)] = k1 + k3
-            stack[rows, pl.ds(pl.multiple_of(col + HALF, LANE), LANE)] = k1 - k2
+            stack[pl.ds(k * 32 + c, 8, stride=pitch), :] = k1 + k3
+            stack[pl.ds(8 * pitch + k * 32 + c, 8, stride=pitch), :] = k1 - k2
 
 
 MESH = pl.DeviceIdType.MESH
@@ -117,7 +114,7 @@
 
 def kernel(
     slots, ranges, offs, starts, lens, x, taper, tabs_hbm, lags_hbm, ones, out,
-    tabs, lags, ext, even, odd, near, wide, diff, stack, stackb, sent, got,
+    tabs, lags, ext, even, odd, far, stack, stackb, sent, got,
     table_sem, halo_send, halo_recv, sum_send, sum_recv,
 ):
     me, z = lax.axis_index("chan"), lax.axis_index("tm")
@@ -237,7 +234,7 @@
                 def _():
                     head_copy(p, 0).wait_recv()
 
-        spectra(ext, place, taper, tabs, ones, even, odd, near, wide, diff)
+        spectra(ext, place, taper, tabs, ones, even, odd, far)
 
     above, below = ranges - 1 - z, z
     most, least = jnp.maximum(above, below), jnp.minimum(above, below)
@@ -290,8 +287,10 @@
     def _(t):
         target = target_of(t)
         last = t == ranges - 1
-        correlate(offs, target * slots, slots, near, wide, diff, stack)
-        stackb[...] = stack[...].astype(jnp.bfloat16)
+        correlate(offs, target * slots, slots, far, stack, rows + 8)
+        for j in range(16):
+            block = stack[pl.ds(j * (rows + 8), rows), :]
+            stackb[:, j * LANE : (j + 1) * LANE] = block.astype(jnp.bfloat16)
 
         @pl.when(t == 0)
         def _():
@@ -373,10 +372,8 @@
             pltpu.VMEM((3, channels, local_len + HALF), jnp.bfloat16),
             pltpu.VMEM((512, HALF), jnp.bfloat16),
             pltpu.VMEM((512, HALF), jnp.bfloat16),
-            pltpu.VMEM((16, 8, 96, LANE), jnp.float32),
-            pltpu.VMEM((16, 8, 96, LANE), jnp.float32),
-            pltpu.VMEM((16, 8, 96, LANE), jnp.float32),
-            pltpu.VMEM((rows, NFFT), jnp.float32),
+            pltpu.VMEM((96 * PITCH, LANE), jnp.float32),
+            pltpu.VMEM((16 * (rows + 8), LANE), jnp.float32),
             pltpu.VMEM((rows, NFFT), jnp.bfloat16),
             pltpu.VMEM((ranges - 1, rows, LAGS), jnp.bfloat16),
             pltpu.VMEM((ranges + 1, rows, LAGS), jnp.bfloat16),

time: 87.3 us -> 77.1 us (0.88)
  Pallas kernels: 84.9 us -> 74.5 us
    pallas_call x1, Pallas kernels: 84.9 us -> 74.5 us  [shards(): pl.pallas_call(lambda *refs: kernel(slots, ranges, *refs), out_shape=jax....]
where the time goes in v4:
time: 77.1 us; the launch traced here: 76.8 us
  Pallas kernels  74.5 us (97%)
  local copies, waits for them, and re-layouts  2.31 us (3%)
    pallas_call x1, Pallas kernels, shards(): pl.pallas_call(lambda *refs: kernel(slots, ranges, *refs), out_shape=jax....  74.5 us
    unnamed x1, local copies, waits for them, and re-layouts  2.31 us

profile of v4, /device:TPU:0, one launch (start us, length us, event | category | flops | bytes accessed | tf_op | source)
XLA Modules:
  0.0 76.8 jit_solution(16400423743686296698)
XLA Ops:
  0.0 74.5 %shard_map.82 = f32[256,1024]{1,0:T(8,128)} custom-call(s32[32]{0:T(128)} %refs_0_.1, s32[4,32]{1,0:T(4,128)} %bitcast.4, s32[4,32]{1,0:T(4,128)} %bitcast.5, bf16[32,16384]{1,0:T(8,128)(2,1)} %refs_3_.1, f32[1,2048]{1,0:T(1,128)} %constant.8.clone.refs_4_, bf16[2,2,1024,512]{3,2,1,0:T(8,128)(2,1)} %constant.9.clone.refs_5_, ...), custom_call_target="tpu_custom_call" | custom-call | tf_op jit(solution)/shard_map/pallas_call | solution.py:364
  74.5 2.3 %copy.10 = f32[8,32,1024]{2,1,0:T(8,128)} copy(f32[8,32,1024]{2,1,0:T(8,128)} %bitcast.3) | data formatting | bytes 2097152
